TPU v7x, 32 devices: a whole 2x2x4 slice. The times are simulated.
32 devices in a mesh: row: 16 (over z, y, x), col: 2 (over core).
Axes of the slice: x: 2, y: 2, z: 4, core: 2. Of those that a mesh axis runs over, the one named last changes fastest.
Arguments:
- vectors: float32 [6144, 64], P(('row', 'col')), may hold values from -6 to 6
- stiff_tiles: float32 [16, 2, 32, 192, 192], P('row', 'col'), may hold values from -0.078125 to 0.078125
- tile_coords: int32 [16, 2, 32, 2], P('row', 'col'), may hold values from 0 to 15, as said below
- tile_valid: int32 [16, 2, 32], P('row', 'col'), may hold values from 0 to 1, as said below
Outputs:
- product: float32 [6144, 64], P(('row', 'col'))
Inputs may be any that keep to these rules, and one draw needn't show every extreme that they name: `tile_coords`: valid entries of a device's list are distinct and come before all padding; each list holds at most 32 valid entries, and some list holds exactly 32. A stored tile may lie on either side of the diagonal. Padding entries hold in-range coordinates. `tile_valid`: at least one entry of each list is valid.
All inputs are finite; a program needn't handle non-finite values.
Results may differ from a plain program's by a relative error of at most 0.0001.
Values sent between devices are 32-bit elements; how exact they have to be, the bound alone decides.
A program may use at most 128 MiB of HBM per device.

v0:
```python
import functools

import jax
import jax.numpy as jnp
from jax import lax
from jax.experimental import pallas as pl
from jax.experimental.pallas import tpu as pltpu
from jax.sharding import PartitionSpec as P

ITERS = 2
MESH = pl.DeviceIdType.MESH
LANES = 128
SPLIT, KEEP, READ = range(3)


def split(value):
    high = value.astype(jnp.bfloat16).astype(jnp.float32)
    return high, value - high


def pack_tall(value):
    half = value.shape[0] // 2
    return jnp.concatenate([value[:half], value[half:]], axis=1)


def spread(packed):
    high, low = split(packed)
    width = packed.shape[1] // 2
    left = lax.broadcasted_iota(jnp.int32, packed.shape, 1) < width
    upper = jnp.where(left, high, pltpu.roll(low, width, 1))
    lower = jnp.where(left, pltpu.roll(high, width, 1), low)
    return jnp.concatenate([upper, lower], axis=0)


def fold_tall(total):
    width = total.shape[1] // 2
    half = total.shape[0] // 2
    folded = total + pltpu.roll(total, width, 1)
    left = lax.broadcasted_iota(jnp.int32, (half, total.shape[1]), 1) < width
    return jnp.where(left, folded[:half], folded[half:])


def unpack_wide(packed, vecs, size):
    main = packed[:vecs].T
    tail = packed[vecs:]
    tail = jnp.concatenate([tail[:, : size - LANES], tail[:, size - LANES :]], axis=0).T
    return jnp.concatenate([main, tail], axis=0)


def kernel(
    rows, cols, planes, kept,
    x_hbm, coords_hbm, valid_hbm, tiles_hbm, out_ref,
    x_ref, coords, valid, table, slot_ref,
    tiles, gath, rowg, rpart, rrecv, zsend, zrecv, z2send, z2recv, lhs, total, parts,
    tile_sem, small_sem, ag_send, ag_recv, at_send, at_recv, cx_send, cx_recv, r1_send, r1_recv, rt_send, rt_recv, r2_send, r2_recv,
    cy_send, cy_recv,
):
    lines = rows // planes
    vecs, size = x_hbm.shape
    half = size // 2
    quarter = half // 2
    row = lax.axis_index("row")
    col = lax.axis_index("col")
    line = row // planes
    plane = row % planes
    up = plane // 2
    side = plane % 2

    load = pltpu.make_async_copy(tiles_hbm, tiles, tile_sem)
    small = [
        pltpu.make_async_copy(src, dst, small_sem.at[i])
        for i, (src, dst) in enumerate(((x_hbm, x_ref), (coords_hbm, coords), (valid_hbm, valid)))
    ]
    for copy in small:
        copy.start()
    load.start()

    def flipped(d):
        if d == 0:
            return plane
        if d == 1:
            return up * 2 + 1 - side
        if d == 2:
            return (1 - up) * 2 + side
        return (1 - up) * 2 + 1 - side

    def line_peer(dz):
        return (((line + dz) % lines) * planes + plane, col)

    def plane_peer(d):
        return (line * planes + flipped(d), col)

    def col_peer(dc):
        return (row, (col + dc) % cols)

    def remote(src, dst, send, recv, where):
        return pltpu.make_async_remote_copy(
            src_ref=src, dst_ref=dst, send_sem=send, recv_sem=recv,
            device_id=where, device_id_type=MESH,
        )

    def ag_line(it, dz):
        return remote(gath.at[it, 0, 0], gath.at[it, dz, 0],
                      ag_send.at[it, dz, 0], ag_recv.at[it, dz, 0], line_peer(dz))

    def ag_plane(it, dz, d):
        return remote(gath.at[it, dz, 0], gath.at[it, dz, d],
                      ag_send.at[it, dz, d], ag_recv.at[it, dz, d], plane_peer(d))

    def ag_turn(it, dz, h):
        part = pl.ds(h * quarter, quarter)
        return remote(gath.at[it, dz, 1 + h, part], gath.at[it, dz, 3, part],
                      at_send.at[it, dz, h], at_recv.at[it, dz, h], plane_peer(2 - h))

    def col_x(it, dc):
        return remote(gath.at[it, 0, 0], rowg.at[it, dc],
                      cx_send.at[it, dc], cx_recv.at[it, dc], col_peer(dc))

    def rs_turn(it, dz, h):
        part = pl.ds(h * quarter, quarter)
        return remote(zsend.at[it, dz, 3, part], zrecv.at[it, dz, 3, part],
                      rt_send.at[it, dz, h], rt_recv.at[it, dz, h], plane_peer(1 + h))

    def rs_plane(it, dz, d):
        return remote(zsend.at[it, dz, d], zrecv.at[it, dz, d],
                      r1_send.at[it, dz, d], r1_recv.at[it, dz, d], plane_peer(d))

    def rs_line(it, dz):
        return remote(z2send.at[it, dz], z2recv.at[it, dz],
                      r2_send.at[it, dz], r2_recv.at[it, dz], line_peer(dz))

    def col_y(it, dc):
        return remote(rpart.at[it, dc], rrecv.at[it, dc],
                      cy_send.at[it, dc], cy_recv.at[it, dc], col_peer(dc))

    barrier = pltpu.get_barrier_semaphore()
    for dz in range(1, lines):
        pl.semaphore_signal(barrier, inc=1, device_id=line_peer(dz), device_id_type=MESH)
    for d in range(1, 3):
        pl.semaphore_signal(barrier, inc=1, device_id=plane_peer(d), device_id_type=MESH)
    for dc in range(1, cols):
        pl.semaphore_signal(barrier, inc=1, device_id=col_peer(dc), device_id_type=MESH)
    for copy in small:
        copy.wait()
    place = jnp.where(valid[...] > 0, coords[0:1, :] * rows + coords[1:2, :], -1)
    spots = (rows * cols, place.shape[1])
    hit = lax.broadcasted_iota(jnp.int32, spots, 0) == jnp.broadcast_to(place, spots)
    found = jnp.max(
        jnp.where(hit, lax.broadcasted_iota(jnp.int32, spots, 1), -1), axis=1, keepdims=True
    )
    table[...] = jnp.broadcast_to(found, table.shape)
    fill = pltpu.make_async_copy(table, slot_ref, small_sem.at[3])
    fill.start()
    gath[0, 0, 0] = pack_tall(
        jnp.concatenate([x_ref[:, :LANES].T, x_ref[:, LANES:].T], axis=0)
    )
    pl.semaphore_wait(barrier, (lines - 1) + 2 + (cols - 1))

    def split_tile(spot):
        slot = slot_ref[spot, 0]
        scale = jnp.where(slot >= 0, 1.0, 0.0).astype(jnp.float32)
        block = tiles[jnp.maximum(slot, 0)] * scale
        high = block.astype(jnp.bfloat16)
        low = (block - high.astype(jnp.float32)).astype(jnp.bfloat16)
        return high, low

    def tile_parts(a, b, mode):
        spot = a * rows + b
        if kept and mode == READ:
            return parts[spot, 0], parts[spot, 1]
        high, low = split_tile(spot)
        if kept and mode == KEEP:
            parts[spot, 0] = high
            parts[spot, 1] = low
        return high, low

    def mirrored(it, dz, d):
        b = ((line + dz) % lines) * planes + flipped(d)
        acc = jnp.zeros((2 * vecs, size), jnp.float32)
        for dc in range(cols):
            a = (col - dc + cols) % cols
            high, low = tile_parts(a, b, KEEP if it == 0 else READ)
            left = lhs[dc]
            if dc == 0 and d == 0:
                left = left * jnp.where(b == row, 0.0, 1.0).astype(jnp.bfloat16)
            acc = acc + jnp.dot(left, high, preferred_element_type=jnp.float32)
            acc = acc + jnp.dot(left, low, preferred_element_type=jnp.float32)
        wide = acc[:vecs] + acc[vecs:]
        tail = wide[:, LANES:]
        return jnp.concatenate(
            [
                wide[:, :LANES],
                jnp.concatenate([tail[: vecs // 2], tail[vecs // 2 :]], axis=1),
            ],
            axis=0,
        )

    def direct(it, dz, *flips):
        sums = [None] * cols
        for d in flips:
            b = ((line - dz + lines) % lines) * planes + flipped(d)
            right = spread(gath[it, dz, d]).astype(jnp.bfloat16)
            for dc in range(cols):
                high, low = tile_parts(
                    (col + dc) % cols, b, SPLIT if it == 0 and d == 0 else READ
                )
                term = jnp.dot(high, right, preferred_element_type=jnp.float32) + jnp.dot(
                    low, right, preferred_element_type=jnp.float32
                )
                sums[dc] = term if sums[dc] is None else sums[dc] + term
        for dc in range(cols):
            total[dc] += sums[dc]

    def product(it):
        for dz in range(1, lines):
            ag_line(it, dz).start()
        for dc in range(1, cols):
            col_x(it, dc).start()
        for d in range(1, 3):
            ag_plane(it, 0, d).start()
        lhs[0] = spread(gath[it, 0, 0]).T.astype(jnp.bfloat16)
        total[...] = jnp.zeros_like(total)

        if it == 0:
            fill.wait()
            load.wait()

        direct(it, 0, 0)
        for dc in range(1, cols):
            col_x(it, dc).wait_recv()
            lhs[dc] = spread(rowg[it, dc]).T.astype(jnp.bfloat16)

        def corner(n, carry):
            dz = (n + 1) % lines
            zsend[it, dz, 3] = mirrored(it, dz, 3)
            for h in range(2):
                rs_turn(it, dz, h).start()
            return carry

        lax.fori_loop(0, lines, corner, 0)

        def group(n, carry):
            dz = (n + 1) % lines
            one = mirrored(it, dz, 1)
            rs_turn(it, dz, 1).wait_recv()
            zsend[it, dz, 1, pl.ds(0, quarter), :] = one[:quarter]
            zsend[it, dz, 1, pl.ds(quarter, quarter), :] = (
                one[quarter:] + zrecv[it, dz, 3, pl.ds(quarter, quarter), :]
            )
            rs_plane(it, dz, 1).start()
            two = mirrored(it, dz, 2)
            rs_turn(it, dz, 0).wait_recv()
            zsend[it, dz, 2, pl.ds(0, quarter), :] = (
                two[:quarter] + zrecv[it, dz, 3, pl.ds(0, quarter), :]
            )
            zsend[it, dz, 2, pl.ds(quarter, quarter), :] = two[quarter:]
            rs_plane(it, dz, 2).start()

            @pl.when(dz > 0)
            def _():
                ag_line(it, dz).wait_recv()
                for d in range(1, 3):
                    ag_plane(it, dz, d).start()

            return carry

        lax.fori_loop(0, lines, group, 0)

        def turn(dz, carry):
            for h in range(2):
                ag_plane(it, dz, 1 + h).wait_recv()
                ag_turn(it, dz, h).start()
            return carry

        def own(n, carry):
            dz = (n + 1) % lines
            mine = mirrored(it, dz, 0)
            turn(n, 0)
            direct(it, n, 1, 2)
            for d in range(1, 3):
                rs_plane(it, dz, d).wait_recv()
            z2send[it, dz] = mine + zrecv[it, dz, 1] + zrecv[it, dz, 2]

            @pl.when(dz > 0)
            def _():
                rs_line(it, dz).start()
                direct(it, dz, 0)

            return carry

        lax.fori_loop(0, lines, own, 0)

        def last(dz, carry):
            for h in range(2):
                ag_turn(it, dz, h).wait_recv()
            direct(it, dz, 3)
            return carry

        lax.fori_loop(0, lines, last, 0)

        for dc in range(1, cols):
            rpart[it, dc] = fold_tall(total[dc])
            col_y(it, dc).start()
        mine = fold_tall(total[0])
        wide = z2send[it, 0]
        for dz in range(1, lines):
            rs_line(it, dz).wait_recv()
            wide = wide + z2recv[it, dz]
        tall = unpack_wide(wide, vecs, size)
        for dc in range(1, cols):
            col_y(it, dc).wait_recv()
            mine = mine + rrecv[it, dc]
        return mine + pack_tall(tall)

    for it in range(ITERS):
        result = product(it)
        if it < ITERS - 1:
            gath[it + 1, 0, 0] = result
        else:
            tall = jnp.concatenate([result[:, :vecs], result[:, vecs:]], axis=0)
            out_ref[:, pl.ds(0, LANES)] = tall[:LANES].T
            out_ref[:, pl.ds(LANES, size - LANES)] = tall[LANES:].T

    def drain(it, carry):
        for dc in range(1, cols):
            col_x(it, dc).wait_send()
            col_y(it, dc).wait_send()
        for dz in range(1, lines):
            ag_line(it, dz).wait_send()
            rs_line(it, dz).wait_send()

        def plane_sends(dz, inner):
            for d in range(1, 3):
                ag_plane(it, dz, d).wait_send()
                rs_plane(it, dz, d).wait_send()
            for h in range(2):
                ag_turn(it, dz, h).wait_send()
                rs_turn(it, dz, h).wait_send()
            return inner

        return lax.fori_loop(0, lines, plane_sends, carry)

    lax.fori_loop(0, ITERS, drain, 0)


def local(rows, cols, vectors, stiff_tiles, tile_coords, tile_valid):
    size, vecs = vectors.shape
    count = stiff_tiles.shape[2]
    planes = 4
    lines = rows // planes
    kept = rows * cols * size * size * 4 <= 16 * 1024 * 1024
    block = (size * vecs // LANES, LANES)
    f32 = jnp.float32
    dma = pltpu.SemaphoreType.DMA
    grid = (ITERS, lines, planes)
    return pl.pallas_call(
        functools.partial(kernel, rows, cols, planes, kept),
        out_shape=jax.ShapeDtypeStruct((vecs, size), f32),
        in_specs=[
            pl.BlockSpec(memory_space=pl.ANY),
            pl.BlockSpec(memory_space=pl.ANY),
            pl.BlockSpec(memory_space=pl.ANY),
            pl.BlockSpec(memory_space=pl.ANY),
        ],
        out_specs=pl.BlockSpec(memory_space=pltpu.VMEM),
        scratch_shapes=[
            pltpu.VMEM((vecs, size), f32),
            pltpu.VMEM((2, count), jnp.int32),
            pltpu.VMEM((1, count), jnp.int32),
            pltpu.VMEM((rows * cols, LANES), jnp.int32),
            pltpu.SMEM((rows * cols, LANES), jnp.int32),
            pltpu.VMEM((count, size, size), f32),
            pltpu.VMEM(grid + block, f32),
            pltpu.VMEM((ITERS, cols) + block, f32),
            pltpu.VMEM((ITERS, cols) + block, f32),
            pltpu.VMEM((ITERS, cols) + block, f32),
            pltpu.VMEM(grid + block, f32),
            pltpu.VMEM(grid + block, f32),
            pltpu.VMEM((ITERS, lines) + block, f32),
            pltpu.VMEM((ITERS, lines) + block, f32),
            pltpu.VMEM((cols, 2 * vecs, size), jnp.bfloat16),
            pltpu.VMEM((cols, size, 2 * vecs), f32),
            pltpu.VMEM((rows * cols if kept else 1, 2, size, size), jnp.bfloat16),
            dma,
            dma((4,)),
            dma(grid), dma(grid),
            dma((ITERS, lines, 2)), dma((ITERS, lines, 2)),
            dma((ITERS, cols)), dma((ITERS, cols)),
            dma(grid), dma(grid),
            dma((ITERS, lines, 2)), dma((ITERS, lines, 2)),
            dma((ITERS, lines)), dma((ITERS, lines)),
            dma((ITERS, cols)), dma((ITERS, cols)),
        ],
        compiler_params=pltpu.CompilerParams(
            collective_id=0, has_side_effects=True, vmem_limit_bytes=48 * 1024 * 1024
        ),
    )(vectors.T, tile_coords[0, 0].T, tile_valid[0], stiff_tiles[0, 0]).T


def solution(mesh):
    placed = (
        P(("row", "col"), None),
        P("row", "col", None, None, None),
        P("row", "col", None, None),
        P("row", "col", None),
    )
    return jax.shard_map(
        functools.partial(local, mesh.shape["row"], mesh.shape["col"]),
        mesh=mesh, in_specs=placed, out_specs=P(("row", "col"), None), check_vma=False,
    )
```

profile of v0, /device:TPU:1, one launch (start us, length us, event | category | flops | bytes accessed | tf_op | source)
XLA Modules:
  0.0 46.1 jit_solution(2280777812281449596)
XLA Ops:
  0.0 0.0 copy-start
  0.0 0.8 %copy-done = f32[192,64]{0,1:T(8,128)S(1)} copy-done((f32[192,64]{0,1:T(8,128)S(1)}, f32[192,64]{0,1:T(8,128)}, u32[]{:S(2)}) %copy-start) | copy-done | bytes 49176
  0.8 0.0 copy-start.1
  0.8 0.7 %copy-done.1 = s32[1,1,32,2]{2,3,1,0:T(2,128)S(1)} copy-done((s32[1,1,32,2]{2,3,1,0:T(2,128)S(1)}, s32[1,1,32,2]{2,3,1,0:T(2,128)}, u32[]{:S(2)}) %copy-start.1) | copy-done | bytes 280
  1.5 0.0 copy-start.2
  1.5 0.7 %copy-done.2 = s32[1,1,32]{2,1,0:T(1,128)S(1)} copy-done((s32[1,1,32]{2,1,0:T(1,128)S(1)}, s32[1,1,32]{2,1,0:T(1,128)}, u32[]{:S(2)}) %copy-start.2) | copy-done | bytes 152
  2.2 43.3 %shard_map.46 = f32[64,192]{1,0:T(8,128)S(1)} custom-call(f32[64,192]{1,0:T(8,128)S(1)} %bitcast.8, s32[2,32]{1,0:T(2,128)S(1)} %bitcast.9, s32[1,32]{1,0:T(1,128)S(1)} %bitcast.10, f32[32,192,192]{2,1,0:T(8,128)} %bitcast.11), custom_call_target="tpu_custom_call" | custom-call | tf_op jit(solution)/shard_map/pallas_call | solution.py:356
  45.5 0.6 %copy.6 = f32[192,64]{0,1:T(8,128)} copy(f32[192,64]{0,1:T(8,128)S(1)} %bitcast.7) | data formatting | bytes 98304
Async XLA Ops:
  0.0 0.8 %copy-start = (f32[192,64]{0,1:T(8,128)S(1)}, f32[192,64]{0,1:T(8,128)}, u32[]{:S(2)}) copy-start(f32[192,64]{0,1:T(8,128)} %param.4) | copy-start | bytes 147460
  0.8 0.7 %copy-start.1 = (s32[1,1,32,2]{2,3,1,0:T(2,128)S(1)}, s32[1,1,32,2]{2,3,1,0:T(2,128)}, u32[]{:S(2)}) copy-start(s32[1,1,32,2]{2,3,1,0:T(2,128)} %param.6) | copy-start | bytes 772
  1.5 0.7 %copy-start.2 = (s32[1,1,32]{2,1,0:T(1,128)S(1)}, s32[1,1,32]{2,1,0:T(1,128)}, u32[]{:S(2)}) copy-start(s32[1,1,32]{2,1,0:T(1,128)} %param.7) | copy-start | bytes 388
where the time goes:
time: 46.3 us; the launch traced here: 46.1 us
  Pallas kernels  43.3 us (94%)
  local copies, waits for them, and re-layouts  2.8 us (6%)
    pallas_call x1, Pallas kernels, local(): pl.pallas_call(functools.partial(kernel, rows, cols, planes, kept), out_s...  43.3 us
    unnamed x7, local copies, waits for them, and re-layouts  2.8 us

commit v1 on v0

--- a/solution.py
+++ b/solution.py
@@ -11,6 +11,21 @@
 MESH = pl.DeviceIdType.MESH
 LANES = 128
 SPLIT, KEEP, READ = range(3)
+ORDER = (
+    ("AP", 2, 0), ("AL", 3, 1), ("AP", 1, 0), ("AP", 1, 1), ("AP", 2, 1), ("AL", 2, 1),
+    ("AL", 1, 1), ("AL", 2, 0), ("LHS",), ("C", 3), ("E", 1, 2), ("C", 2), ("E", 3, 1),
+    ("AL", 1, 0), ("C", 1), ("AL", 3, 0), ("AF", 1, 2, 0), ("AT", 0, 1), ("AF", 1, 1, 0),
+    ("AT", 0, 0), ("E", 3, 2), ("E", 2, 1), ("E", 1, 1), ("D", 0, 1), ("L", 3, 2), ("L", 3, 1),
+    ("AF", 2, 1, 1), ("AF", 1, 1, 1), ("E", 2, 2), ("L", 2, 1), ("L", 2, 2), ("M", 3),
+    ("AF", 2, 1, 0), ("AF", 1, 2, 1), ("AF", 2, 2, 1), ("AF", 2, 2, 0), ("E", 0, 2),
+    ("L", 1, 2), ("AF", 3, 2, 0), ("C", 0), ("L", 1, 1), ("M", 1), ("AF", 3, 1, 0),
+    ("RL", 1, 1), ("AT", 1, 1), ("E", 0, 1), ("AF", 3, 2, 1), ("RL", 3, 0), ("AF", 3, 1, 1),
+    ("S", 2, 0), ("RL", 3, 1), ("M", 2), ("D", 1, 0), ("D", 3, 0), ("RL", 2, 0), ("S", 1, 0),
+    ("RL", 1, 0), ("AT", 1, 0), ("RL", 2, 1), ("AT", 2, 0), ("D", 1, 2), ("AT", 2, 1),
+    ("D", 1, 1), ("AT", 3, 0), ("D", 2, 1), ("AT", 3, 1), ("S", 2, 1), ("S", 1, 1), ("M", 0),
+    ("D", 0, 0), ("D", 3, 2), ("D", 0, 2), ("D", 2, 0), ("D", 2, 2), ("D", 0, 3), ("D", 1, 3),
+    ("D", 3, 1), ("D", 2, 3), ("G",), ("FR",), ("D", 3, 3),
+)
 
 
 def split(value):
@@ -84,8 +99,15 @@
             return (1 - up) * 2 + side
         return (1 - up) * 2 + 1 - side
 
+    def across(dz):
+        spot, bit = 0, 1
+        while bit < lines:
+            spot = spot + (line // bit + dz // bit) % 2 * bit
+            bit *= 2
+        return spot
+
     def line_peer(dz):
-        return (((line + dz) % lines) * planes + plane, col)
+        return (across(dz) * planes + plane, col)
 
     def plane_peer(d):
         return (line * planes + flipped(d), col)
@@ -99,13 +121,41 @@
             device_id=where, device_id_type=MESH,
         )
 
+    def piece(p):
+        return pl.ds(p % 2 * quarter, quarter)
+
     def ag_line(it, dz):
         return remote(gath.at[it, 0, 0], gath.at[it, dz, 0],
-                      ag_send.at[it, dz, 0], ag_recv.at[it, dz, 0], line_peer(dz))
+                      ag_send.at[it, dz, 0, 0], ag_recv.at[it, dz, 0, 0], line_peer(dz))
 
     def ag_plane(it, dz, d):
         return remote(gath.at[it, dz, 0], gath.at[it, dz, d],
-                      ag_send.at[it, dz, d], ag_recv.at[it, dz, d], plane_peer(d))
+                      ag_send.at[it, dz, d, 0], ag_recv.at[it, dz, d, 0], plane_peer(d))
+
+    def ag_line_half(it, dz, p):
+        part = piece(p)
+        return remote(gath.at[it, 0, 0, part], gath.at[it, dz, 0, part],
+                      ag_send.at[it, dz, 0, p], ag_recv.at[it, dz, 0, p], line_peer(dz))
+
+    def ag_plane_half(it, dz, d, q):
+        part = piece(d - 1 + q)
+        return remote(gath.at[it, dz, 0, part], gath.at[it, dz, d, part],
+                      ag_send.at[it, dz, d, q], ag_recv.at[it, dz, d, q], plane_peer(d))
+
+    def ag_pair_half(it, d, q):
+        part = piece(d - 1 + q)
+        return remote(gath.at[it, 0, d, part], gath.at[it, 1, d, part],
+                      ag_send.at[it, 1, d, q], ag_recv.at[it, 1, d, q], line_peer(1))
+
+    def rs_pair(it, d, q):
+        part = piece(d - 1 + q)
+        return remote(zsend.at[it, 1, d, part], zrecv.at[it, 1, d, part],
+                      r1_send.at[it, 1, d, q], r1_recv.at[it, 1, d, q], line_peer(1))
+
+    def rs_line_half(it, dz, p):
+        part = piece(p)
+        return remote(z2send.at[it, dz, part], z2recv.at[it, dz, part],
+                      r2_send.at[it, dz, p], r2_recv.at[it, dz, p], line_peer(dz))
 
     def ag_turn(it, dz, h):
         part = pl.ds(h * quarter, quarter)
@@ -121,18 +171,25 @@
         return remote(zsend.at[it, dz, 3, part], zrecv.at[it, dz, 3, part],
                       rt_send.at[it, dz, h], rt_recv.at[it, dz, h], plane_peer(1 + h))
 
-    def rs_plane(it, dz, d):
-        return remote(zsend.at[it, dz, d], zrecv.at[it, dz, d],
-                      r1_send.at[it, dz, d], r1_recv.at[it, dz, d], plane_peer(d))
+    def rs_plane(it, dz, d, late):
+        part = pl.ds((d - 1 + late) % 2 * quarter, quarter)
+        return remote(zsend.at[it, dz, d, part], zrecv.at[it, dz, d, part],
+                      r1_send.at[it, dz, d, late], r1_recv.at[it, dz, d, late], plane_peer(d))
 
     def rs_line(it, dz):
         return remote(z2send.at[it, dz], z2recv.at[it, dz],
-                      r2_send.at[it, dz], r2_recv.at[it, dz], line_peer(dz))
+                      r2_send.at[it, dz, 0], r2_recv.at[it, dz, 0], line_peer(dz))
 
     def col_y(it, dc):
         return remote(rpart.at[it, dc], rrecv.at[it, dc],
                       cy_send.at[it, dc], cy_recv.at[it, dc], col_peer(dc))
 
+    def col_s(it):
+        return remote(rpart.at[it, 0], rrecv.at[it, 0],
+                      cy_send.at[it, 0], cy_recv.at[it, 0], col_peer(1))
+
+    paired = cols == 2
+    planned = paired and lines == 4 and kept
     barrier = pltpu.get_barrier_semaphore()
     for dz in range(1, lines):
         pl.semaphore_signal(barrier, inc=1, device_id=line_peer(dz), device_id_type=MESH)
@@ -154,7 +211,6 @@
     gath[0, 0, 0] = pack_tall(
         jnp.concatenate([x_ref[:, :LANES].T, x_ref[:, LANES:].T], axis=0)
     )
-    pl.semaphore_wait(barrier, (lines - 1) + 2 + (cols - 1))
 
     def split_tile(spot):
         slot = slot_ref[spot, 0]
@@ -174,14 +230,19 @@
             parts[spot, 1] = low
         return high, low
 
-    def mirrored(it, dz, d):
-        b = ((line + dz) % lines) * planes + flipped(d)
+    def mirrored(it, dz, d, mode=None):
+        if mode is None:
+            mode = KEEP if it == 0 else READ
+        known = isinstance(dz, int)
+        b = across(dz) * planes + flipped(d)
         acc = jnp.zeros((2 * vecs, size), jnp.float32)
         for dc in range(cols):
+            if known and dz == 0 and d == 0 and dc == 0:
+                continue
             a = (col - dc + cols) % cols
-            high, low = tile_parts(a, b, KEEP if it == 0 else READ)
+            high, low = tile_parts(a, b, mode)
             left = lhs[dc]
-            if dc == 0 and d == 0:
+            if dc == 0 and d == 0 and not known:
                 left = left * jnp.where(b == row, 0.0, 1.0).astype(jnp.bfloat16)
             acc = acc + jnp.dot(left, high, preferred_element_type=jnp.float32)
             acc = acc + jnp.dot(left, low, preferred_element_type=jnp.float32)
@@ -195,10 +256,17 @@
             axis=0,
         )
 
+    def term(dz, d, dc, right, mode):
+        b = across(dz) * planes + flipped(d)
+        high, low = tile_parts((col + dc) % cols, b, mode)
+        return jnp.dot(high, right, preferred_element_type=jnp.float32) + jnp.dot(
+            low, right, preferred_element_type=jnp.float32
+        )
+
     def direct(it, dz, *flips):
         sums = [None] * cols
         for d in flips:
-            b = ((line - dz + lines) % lines) * planes + flipped(d)
+            b = across(dz) * planes + flipped(d)
             right = spread(gath[it, dz, d]).astype(jnp.bfloat16)
             for dc in range(cols):
                 high, low = tile_parts(
@@ -211,27 +279,209 @@
         for dc in range(cols):
             total[dc] += sums[dc]
 
+    def begin(it):
+        lhs[0] = spread(gath[it, 0, 0]).T.astype(jnp.bfloat16)
+        total[...] = jnp.zeros_like(total)
+        direct(it, 0, 0)
+
+    seen = set()
+
+    def access(it, dz, d):
+        first = (dz, d) not in seen
+        seen.add((dz, d))
+        return KEEP if first else READ
+
+    def blocked(it, dz, d, fresh=False):
+        right = spread(gath[it, dz, d]).astype(jnp.bfloat16)
+        mode = access(it, dz, d)
+        for dc in range(cols):
+            part = term(dz, d, dc, right, mode)
+            if fresh:
+                total[dc] = part
+            else:
+                total[dc] += part
+
+    fill.wait()
+    load.wait()
+    if planned:
+        blocked(0, 0, 0, True)
+    else:
+        begin(0)
+    pl.semaphore_wait(barrier, (lines - 1) + 2 + (cols - 1))
+
+    def finish_sends(it):
+        def along(dz, carry):
+            for p in range(2):
+                ag_line_half(it, dz, p).wait_send()
+                rs_line_half(it, dz, p).wait_send()
+            return carry
+
+        def within(dz, carry):
+            for h in range(2):
+                for d in range(1, 3):
+                    ag_plane_half(it, dz, d, h).wait_send()
+                    rs_plane(it, dz, d, h).wait_send()
+                ag_turn(it, dz, h).wait_send()
+                rs_turn(it, dz, h).wait_send()
+            return carry
+
+        lax.fori_loop(1, lines, along, 0)
+        lax.fori_loop(0, lines, within, 0)
+
+    def ordered(it):
+        arrived = set()
+        opening = next(task for task in ORDER if task[0] == "D")
+
+        def once(copy, *key):
+            if key not in arrived:
+                arrived.add(key)
+                copy(it, *key[1:]).wait_recv()
+
+        def gathered(dz, d, q):
+            if dz == 1:
+                once(lambda it, dz, d, q: ag_pair_half(it, d, q), "ap", dz, d, q)
+            else:
+                once(ag_plane_half, "ap", dz, d, q)
+
+        def reduced(dz, d, q):
+            once(rs_plane, "rp", dz, d, q)
+
+        def mirror(dz, d):
+            return mirrored(it, dz, d, access(it, dz, d))
+
+        if it == 0:
+            for dc in range(1, cols):
+                col_x(it, dc).start()
+        for place, task in enumerate(ORDER):
+            kind, args = task[0], task[1:]
+            if it > 0 and place == len(ORDER) // 2:
+                finish_sends(it - 1)
+            if kind == "AL":
+                ag_line_half(it, *args).start()
+            elif kind == "AP":
+                ag_plane_half(it, 0, *args).start()
+            elif kind == "LHS":
+                lhs[0] = spread(gath[it, 0, 0]).T.astype(jnp.bfloat16)
+                if it == 0:
+                    col_x(it, 1).wait_recv()
+                    near = rowg[it, 1]
+                else:
+                    col_s(it - 1).wait_recv()
+                    near = rrecv[it - 1, 0] + rpart[it - 1, 1]
+                lhs[1] = spread(near).T.astype(jnp.bfloat16)
+            elif kind == "C":
+                dz, = args
+                zsend[it, dz, 3] = mirror(dz, 3)
+                for h in range(2):
+                    rs_turn(it, dz, h).start()
+            elif kind == "E":
+                dz, d = args
+                zsend[it, dz, d] = mirror(dz, d)
+                if dz == 1:
+                    rs_pair(it, d, 0).start()
+                elif dz > 1:
+                    rs_plane(it, dz, d, 0).start()
+            elif kind == "L":
+                dz, d = args
+                once(rs_turn, "rt", dz, d % 2)
+                zsend[it, dz, d, piece(d)] += zrecv[it, dz, 3, piece(d)]
+                if dz == 1:
+                    rs_pair(it, d, 1).start()
+                else:
+                    rs_plane(it, dz, d, 1).start()
+            elif kind == "S":
+                d, q = args
+                part = piece(d - 1 + q)
+                once(lambda it, dz, d, q: rs_pair(it, d, q), "rp", 1, d, q)
+                more = zrecv[it, 1, d, part]
+                if q == 1:
+                    once(rs_turn, "rt", 0, d % 2)
+                    more = more + zrecv[it, 0, 3, part]
+                zsend[it, 0, d, part] += more
+                rs_plane(it, 0, d, q).start()
+            elif kind == "M":
+                dz, = args
+                z2send[it, dz] = mirror(dz, 0)
+            elif kind == "RL":
+                dz, p = args
+                part = piece(p)
+                if dz > 1:
+                    reduced(dz, 1, p)
+                    reduced(dz, 2, 1 - p)
+                    z2send[it, dz, part] += zrecv[it, dz, 1, part] + zrecv[it, dz, 2, part]
+                rs_line_half(it, dz, p).start()
+            elif kind == "G":
+                for d in range(1, 3):
+                    for q in range(2):
+                        reduced(0, d, q)
+                z2send[it, 0] += zrecv[it, 0, 1] + zrecv[it, 0, 2]
+            elif kind == "FR":
+                wide = z2send[it, 0]
+                for dz in range(1, lines):
+                    for p in range(2):
+                        once(rs_line_half, "rl", dz, p)
+                    wide = wide + z2recv[it, dz]
+                z2send[it, 0] = pack_tall(unpack_wide(wide, vecs, size))
+            elif kind == "AF":
+                dz, d, q = args
+                if dz == 1:
+                    gathered(0, d, q)
+                    ag_pair_half(it, d, q).start()
+                else:
+                    once(ag_line_half, "al", dz, (d - 1 + q) % 2)
+                    ag_plane_half(it, dz, d, q).start()
+            elif kind == "AT":
+                dz, h = args
+                gathered(dz, 1 + h, 0)
+                ag_turn(it, dz, h).start()
+            elif it > 0 or args != (0, 0):
+                dz, d = args
+                if place == len(ORDER) - 1 and it == ITERS - 1:
+                    finish_sends(it)
+                if d == 0 and dz > 0:
+                    for p in range(2):
+                        once(ag_line_half, "al", dz, p)
+                elif d in (1, 2):
+                    for q in range(2):
+                        gathered(dz, d, q)
+                elif d == 3:
+                    for h in range(2):
+                        once(ag_turn, "at", dz, h)
+                if place < len(ORDER) - 1:
+                    blocked(it, dz, d, it > 0 and task == opening)
+        right = spread(gath[it, dz, d]).astype(jnp.bfloat16)
+        mode = access(it, dz, d)
+        rpart[it, 1] = fold_tall(total[1] + term(dz, d, 1, right, mode))
+        col_y(it, 1).start()
+        mine = fold_tall(total[0] + term(dz, d, 0, right, mode)) + z2send[it, 0]
+        if it < ITERS - 1:
+            rpart[it, 0] = mine
+            col_s(it).start()
+        col_y(it, 1).wait_recv()
+        return mine + rrecv[it, 1]
+
     def product(it):
         for dz in range(1, lines):
             ag_line(it, dz).start()
-        for dc in range(1, cols):
-            col_x(it, dc).start()
+        fresh = it == 0 or not paired
+        if fresh:
+            for dc in range(1, cols):
+                col_x(it, dc).start()
         for d in range(1, 3):
             ag_plane(it, 0, d).start()
-        lhs[0] = spread(gath[it, 0, 0]).T.astype(jnp.bfloat16)
-        total[...] = jnp.zeros_like(total)
-
-        if it == 0:
-            fill.wait()
-            load.wait()
-
-        direct(it, 0, 0)
-        for dc in range(1, cols):
-            col_x(it, dc).wait_recv()
-            lhs[dc] = spread(rowg[it, dc]).T.astype(jnp.bfloat16)
+        if it > 0:
+            begin(it)
+        if fresh:
+            for dc in range(1, cols):
+                col_x(it, dc).wait_recv()
+                lhs[dc] = spread(rowg[it, dc]).T.astype(jnp.bfloat16)
+        else:
+            col_s(it - 1).wait_recv()
+            near = rrecv[it - 1, 0] + rpart[it - 1, 1]
+            lhs[1] = spread(near).T.astype(jnp.bfloat16)
 
         def corner(n, carry):
-            dz = (n + 1) % lines
+            dz = lines - 1 - n
             zsend[it, dz, 3] = mirrored(it, dz, 3)
             for h in range(2):
                 rs_turn(it, dz, h).start()
@@ -239,56 +489,57 @@
 
         lax.fori_loop(0, lines, corner, 0)
 
-        def group(n, carry):
-            dz = (n + 1) % lines
-            one = mirrored(it, dz, 1)
-            rs_turn(it, dz, 1).wait_recv()
-            zsend[it, dz, 1, pl.ds(0, quarter), :] = one[:quarter]
-            zsend[it, dz, 1, pl.ds(quarter, quarter), :] = (
-                one[quarter:] + zrecv[it, dz, 3, pl.ds(quarter, quarter), :]
-            )
-            rs_plane(it, dz, 1).start()
-            two = mirrored(it, dz, 2)
-            rs_turn(it, dz, 0).wait_recv()
-            zsend[it, dz, 2, pl.ds(0, quarter), :] = (
-                two[:quarter] + zrecv[it, dz, 3, pl.ds(0, quarter), :]
-            )
-            zsend[it, dz, 2, pl.ds(quarter, quarter), :] = two[quarter:]
-            rs_plane(it, dz, 2).start()
-
-            @pl.when(dz > 0)
-            def _():
-                ag_line(it, dz).wait_recv()
-                for d in range(1, 3):
-                    ag_plane(it, dz, d).start()
-
+        def early(n, carry):
+            dz = (lines - n) % lines
+            for d in range(1, 3):
+                zsend[it, dz, d] = mirrored(it, dz, d)
+                rs_plane(it, dz, d, 0).start()
             return carry
 
-        lax.fori_loop(0, lines, group, 0)
-
-        def turn(dz, carry):
+        def late(dz):
+            for d in range(1, 3):
+                part = pl.ds(d % 2 * quarter, quarter)
+                rs_turn(it, dz, d % 2).wait_recv()
+                zsend[it, dz, d, part] += zrecv[it, dz, 3, part]
+                rs_plane(it, dz, d, 1).start()
+
+        def forward(dz, carry):
+            back = lines - dz
+            late(back)
+            ag_line(it, dz).wait_recv()
+            for d in range(1, 3):
+                ag_plane(it, dz, d).start()
+            z2send[it, back] = mirrored(it, back, 0)
+            direct(it, dz, 0)
+            return carry
+
+        def turn(dz):
             for h in range(2):
                 ag_plane(it, dz, 1 + h).wait_recv()
                 ag_turn(it, dz, h).start()
+
+        def gather_plane(dz):
+            for d in range(1, 3):
+                for k in range(2):
+                    rs_plane(it, dz, d, k).wait_recv()
+            z2send[it, dz] += zrecv[it, dz, 1] + zrecv[it, dz, 2]
+
+        def settle(dz, carry):
+            gather_plane(lines - dz)
+            rs_line(it, lines - dz).start()
+            turn(dz)
+            direct(it, dz, 1, 2)
             return carry
 
-        def own(n, carry):
-            dz = (n + 1) % lines
-            mine = mirrored(it, dz, 0)
-            turn(n, 0)
-            direct(it, n, 1, 2)
-            for d in range(1, 3):
-                rs_plane(it, dz, d).wait_recv()
-            z2send[it, dz] = mine + zrecv[it, dz, 1] + zrecv[it, dz, 2]
-
-            @pl.when(dz > 0)
-            def _():
-                rs_line(it, dz).start()
-                direct(it, dz, 0)
-
-            return carry
-
-        lax.fori_loop(0, lines, own, 0)
+        lax.fori_loop(1, lines, early, 0)
+        lax.fori_loop(1, lines, forward, 0)
+        early(0, 0)
+        late(0)
+        z2send[it, 0] = mirrored(it, 0, 0)
+        turn(0)
+        direct(it, 0, 1, 2)
+        lax.fori_loop(1, lines, settle, 0)
+        gather_plane(0)
 
         def last(dz, carry):
             for h in range(2):
@@ -306,14 +557,17 @@
         for dz in range(1, lines):
             rs_line(it, dz).wait_recv()
             wide = wide + z2recv[it, dz]
-        tall = unpack_wide(wide, vecs, size)
+        mine = mine + pack_tall(unpack_wide(wide, vecs, size))
+        if paired and it < ITERS - 1:
+            rpart[it, 0] = mine
+            col_s(it).start()
         for dc in range(1, cols):
             col_y(it, dc).wait_recv()
             mine = mine + rrecv[it, dc]
-        return mine + pack_tall(tall)
+        return mine
 
     for it in range(ITERS):
-        result = product(it)
+        result = ordered(it) if planned else product(it)
         if it < ITERS - 1:
             gath[it + 1, 0, 0] = result
         else:
@@ -321,10 +575,15 @@
             out_ref[:, pl.ds(0, LANES)] = tall[:LANES].T
             out_ref[:, pl.ds(LANES, size - LANES)] = tall[LANES:].T
 
+    for it in range(ITERS):
+        for dc in range(1, cols):
+            if it == 0 or not paired:
+                col_x(it, dc).wait_send()
+            col_y(it, dc).wait_send()
+        if paired and it < ITERS - 1:
+            col_s(it).wait_send()
+
     def drain(it, carry):
-        for dc in range(1, cols):
-            col_x(it, dc).wait_send()
-            col_y(it, dc).wait_send()
         for dz in range(1, lines):
             ag_line(it, dz).wait_send()
             rs_line(it, dz).wait_send()
@@ -332,7 +591,8 @@
         def plane_sends(dz, inner):
             for d in range(1, 3):
                 ag_plane(it, dz, d).wait_send()
-                rs_plane(it, dz, d).wait_send()
+                for k in range(2):
+                    rs_plane(it, dz, d, k).wait_send()
             for h in range(2):
                 ag_turn(it, dz, h).wait_send()
                 rs_turn(it, dz, h).wait_send()
@@ -340,7 +600,8 @@
 
         return lax.fori_loop(0, lines, plane_sends, carry)
 
-    lax.fori_loop(0, ITERS, drain, 0)
+    if not planned:
+        lax.fori_loop(0, ITERS, drain, 0)
 
 
 def local(rows, cols, vectors, stiff_tiles, tile_coords, tile_valid):
@@ -383,16 +644,16 @@
             pltpu.VMEM((rows * cols if kept else 1, 2, size, size), jnp.bfloat16),
             dma,
             dma((4,)),
-            dma(grid), dma(grid),
+            dma(grid + (2,)), dma(grid + (2,)),
             dma((ITERS, lines, 2)), dma((ITERS, lines, 2)),
             dma((ITERS, cols)), dma((ITERS, cols)),
-            dma(grid), dma(grid),
+            dma(grid + (2,)), dma(grid + (2,)),
             dma((ITERS, lines, 2)), dma((ITERS, lines, 2)),
-            dma((ITERS, lines)), dma((ITERS, lines)),
+            dma((ITERS, lines, 2)), dma((ITERS, lines, 2)),
             dma((ITERS, cols)), dma((ITERS, cols)),
         ],
         compiler_params=pltpu.CompilerParams(
-            collective_id=0, has_side_effects=True, vmem_limit_bytes=48 * 1024 * 1024
+            collective_id=0, has_side_effects=True, vmem_limit_bytes=60 * 1024 * 1024
         ),
     )(vectors.T, tile_coords[0, 0].T, tile_valid[0], stiff_tiles[0, 0]).T
 

time: 46.3 us -> 42.4 us (0.916)
  Pallas kernels: 43.3 us -> 40.8 us
  local copies, waits for them, and re-layouts: 2.8 us -> 1.47 us
    pallas_call x1, Pallas kernels: 43.3 us -> 40.8 us  [local(): pl.pallas_call(functools.partial(kernel, rows, cols, planes, kept), out_s...]
    unnamed x7 -> x1, local copies, waits for them, and re-layouts: 2.8 us -> 1.47 us
where the time goes in v1:
time: 42.4 us; the launch traced here: 42.3 us
  Pallas kernels  40.8 us (96%)
  local copies, waits for them, and re-layouts  1.47 us (3%)
    pallas_call x1, Pallas kernels, local(): pl.pallas_call(functools.partial(kernel, rows, cols, planes, kept), out_s...  40.8 us
    unnamed x1, local copies, waits for them, and re-layouts  1.47 us

profile of v1, /device:TPU:1, one launch (start us, length us, event | category | flops | bytes accessed | tf_op | source)
XLA Modules:
  0.0 42.3 jit_solution(3069404888425566619)
XLA Ops:
  0.0 40.8 %shard_map.46 = f32[64,192]{1,0:T(8,128)} custom-call(f32[64,192]{1,0:T(8,128)} %bitcast.9, s32[2,32]{1,0:T(2,128)} %bitcast.10, s32[1,32]{1,0:T(1,128)} %bitcast.11, f32[32,192,192]{2,1,0:T(8,128)} %bitcast.7), custom_call_target="tpu_custom_call" | custom-call | tf_op jit(solution)/shard_map/pallas_call | solution.py:617
  40.8 1.5 %copy.6 = f32[192,64]{0,1:T(8,128)} copy(f32[192,64]{0,1:T(8,128)} %bitcast.8) | data formatting | bytes 98304

commit v2 on v1

--- a/solution.py
+++ b/solution.py
@@ -10,7 +10,8 @@
 ITERS = 2
 MESH = pl.DeviceIdType.MESH
 LANES = 128
-SPLIT, KEEP, READ = range(3)
+CHUNKS = 4
+PAIR = True
 ORDER = (
     ("AP", 2, 0), ("AL", 3, 1), ("AP", 1, 0), ("AP", 1, 1), ("AP", 2, 1), ("AL", 2, 1),
     ("AL", 1, 1), ("AL", 2, 0), ("LHS",), ("C", 3), ("E", 1, 2), ("C", 2), ("E", 3, 1),
@@ -66,8 +67,8 @@
     rows, cols, planes, kept,
     x_hbm, coords_hbm, valid_hbm, tiles_hbm, out_ref,
     x_ref, coords, valid, table, slot_ref,
-    tiles, gath, rowg, rpart, rrecv, zsend, zrecv, z2send, z2recv, lhs, total, parts,
-    tile_sem, small_sem, ag_send, ag_recv, at_send, at_recv, cx_send, cx_recv, r1_send, r1_recv, rt_send, rt_recv, r2_send, r2_recv,
+    tiles, gath, rowg, rpart, rrecv, zsend, zrecv, z2send, z2recv, lhs, total, parts, stack, tile_sem,
+    small_sem, ag_send, ag_recv, at_send, at_recv, cx_send, cx_recv, r1_send, r1_recv, rt_send, rt_recv, r2_send, r2_recv,
     cy_send, cy_recv,
 ):
     lines = rows // planes
@@ -81,14 +82,19 @@
     up = plane // 2
     side = plane % 2
 
-    load = pltpu.make_async_copy(tiles_hbm, tiles, tile_sem)
+    count = tiles.shape[0]
+    share = count // CHUNKS
+    spans = [
+        pl.ds(i * share, share if i < CHUNKS - 1 else count - i * share) for i in range(CHUNKS)
+    ]
+    loads = [
+        pltpu.make_async_copy(tiles_hbm.at[span], tiles.at[span], tile_sem.at[i])
+        for i, span in enumerate(spans)
+    ]
     small = [
         pltpu.make_async_copy(src, dst, small_sem.at[i])
         for i, (src, dst) in enumerate(((x_hbm, x_ref), (coords_hbm, coords), (valid_hbm, valid)))
     ]
-    for copy in small:
-        copy.start()
-    load.start()
 
     def flipped(d):
         if d == 0:
@@ -189,7 +195,7 @@
                       cy_send.at[it, 0], cy_recv.at[it, 0], col_peer(1))
 
     paired = cols == 2
-    planned = paired and lines == 4 and kept
+    planned = kept
     barrier = pltpu.get_barrier_semaphore()
     for dz in range(1, lines):
         pl.semaphore_signal(barrier, inc=1, device_id=line_peer(dz), device_id_type=MESH)
@@ -197,6 +203,10 @@
         pl.semaphore_signal(barrier, inc=1, device_id=plane_peer(d), device_id_type=MESH)
     for dc in range(1, cols):
         pl.semaphore_signal(barrier, inc=1, device_id=col_peer(dc), device_id_type=MESH)
+    for copy in small:
+        copy.start()
+    for load in loads:
+        load.start()
     for copy in small:
         copy.wait()
     place = jnp.where(valid[...] > 0, coords[0:1, :] * rows + coords[1:2, :], -1)
@@ -220,32 +230,11 @@
         low = (block - high.astype(jnp.float32)).astype(jnp.bfloat16)
         return high, low
 
-    def tile_parts(a, b, mode):
-        spot = a * rows + b
-        if kept and mode == READ:
-            return parts[spot, 0], parts[spot, 1]
-        high, low = split_tile(spot)
-        if kept and mode == KEEP:
-            parts[spot, 0] = high
-            parts[spot, 1] = low
-        return high, low
-
-    def mirrored(it, dz, d, mode=None):
-        if mode is None:
-            mode = KEEP if it == 0 else READ
-        known = isinstance(dz, int)
-        b = across(dz) * planes + flipped(d)
-        acc = jnp.zeros((2 * vecs, size), jnp.float32)
-        for dc in range(cols):
-            if known and dz == 0 and d == 0 and dc == 0:
-                continue
-            a = (col - dc + cols) % cols
-            high, low = tile_parts(a, b, mode)
-            left = lhs[dc]
-            if dc == 0 and d == 0 and not known:
-                left = left * jnp.where(b == row, 0.0, 1.0).astype(jnp.bfloat16)
-            acc = acc + jnp.dot(left, high, preferred_element_type=jnp.float32)
-            acc = acc + jnp.dot(left, low, preferred_element_type=jnp.float32)
+    def stored(a, b):
+        slot = slot_ref[a * rows + b, 0]
+        return jnp.where(slot >= 0, slot, count)
+
+    def folded(acc):
         wide = acc[:vecs] + acc[vecs:]
         tail = wide[:, LANES:]
         return jnp.concatenate(
@@ -256,12 +245,33 @@
             axis=0,
         )
 
-    def term(dz, d, dc, right, mode):
+    def mirrored(it, dz, d):
         b = across(dz) * planes + flipped(d)
-        high, low = tile_parts((col + dc) % cols, b, mode)
-        return jnp.dot(high, right, preferred_element_type=jnp.float32) + jnp.dot(
-            low, right, preferred_element_type=jnp.float32
-        )
+        if planned:
+            spots = [stored(a, b) for a in range(cols)]
+            if dz == 0 and d == 0:
+                spots = [jnp.where(col == a, count, spots[a]) for a in range(cols)]
+            right = jnp.concatenate([parts[spot] for spot in spots], axis=0)
+            return folded(jnp.dot(stack[...], right, preferred_element_type=jnp.float32))
+        acc = jnp.zeros((2 * vecs, size), jnp.float32)
+        for dc in range(cols):
+            high, low = split_tile((col - dc + cols) % cols * rows + b)
+            left = lhs[dc]
+            if dc == 0 and d == 0:
+                left = left * jnp.where(b == row, 0.0, 1.0).astype(jnp.bfloat16)
+            acc = acc + jnp.dot(left, high, preferred_element_type=jnp.float32)
+            acc = acc + jnp.dot(left, low, preferred_element_type=jnp.float32)
+        return folded(acc)
+
+    def terms(dz, d, right, *shifts):
+        b = across(dz) * planes + flipped(d)
+        result = []
+        for dc in shifts:
+            both = jnp.dot(
+                parts[stored((col + dc) % cols, b)], right, preferred_element_type=jnp.float32
+            )
+            result.append(both[:size] + both[size:])
+        return result
 
     def direct(it, dz, *flips):
         sums = [None] * cols
@@ -269,9 +279,7 @@
             b = across(dz) * planes + flipped(d)
             right = spread(gath[it, dz, d]).astype(jnp.bfloat16)
             for dc in range(cols):
-                high, low = tile_parts(
-                    (col + dc) % cols, b, SPLIT if it == 0 and d == 0 else READ
-                )
+                high, low = split_tile((col + dc) % cols * rows + b)
                 term = jnp.dot(high, right, preferred_element_type=jnp.float32) + jnp.dot(
                     low, right, preferred_element_type=jnp.float32
                 )
@@ -284,28 +292,35 @@
         total[...] = jnp.zeros_like(total)
         direct(it, 0, 0)
 
-    seen = set()
-
-    def access(it, dz, d):
-        first = (dz, d) not in seen
-        seen.add((dz, d))
-        return KEEP if first else READ
-
     def blocked(it, dz, d, fresh=False):
         right = spread(gath[it, dz, d]).astype(jnp.bfloat16)
-        mode = access(it, dz, d)
-        for dc in range(cols):
-            part = term(dz, d, dc, right, mode)
+        for dc, part in enumerate(terms(dz, d, right, *range(cols))):
             if fresh:
                 total[dc] = part
             else:
                 total[dc] += part
 
-    fill.wait()
-    load.wait()
     if planned:
+        parts[count] = jnp.zeros((2 * size, size), jnp.bfloat16)
+        for i, load in enumerate(loads):
+            load.wait()
+
+            def cut(slot, carry):
+                block = tiles[slot]
+                high = block.astype(jnp.bfloat16)
+                parts[slot, pl.ds(0, size)] = high
+                parts[slot, pl.ds(size, size)] = (block - high.astype(jnp.float32)).astype(
+                    jnp.bfloat16
+                )
+                return carry
+
+            lax.fori_loop(i * share, (i + 1) * share, cut, 0)
+        fill.wait()
         blocked(0, 0, 0, True)
     else:
+        for load in loads:
+            load.wait()
+        fill.wait()
         begin(0)
     pl.semaphore_wait(barrier, (lines - 1) + 2 + (cols - 1))
 
@@ -338,16 +353,13 @@
                 copy(it, *key[1:]).wait_recv()
 
         def gathered(dz, d, q):
-            if dz == 1:
+            if PAIR and dz == 1:
                 once(lambda it, dz, d, q: ag_pair_half(it, d, q), "ap", dz, d, q)
             else:
                 once(ag_plane_half, "ap", dz, d, q)
 
         def reduced(dz, d, q):
             once(rs_plane, "rp", dz, d, q)
-
-        def mirror(dz, d):
-            return mirrored(it, dz, d, access(it, dz, d))
 
         if it == 0:
             for dc in range(1, cols):
@@ -361,31 +373,34 @@
             elif kind == "AP":
                 ag_plane_half(it, 0, *args).start()
             elif kind == "LHS":
-                lhs[0] = spread(gath[it, 0, 0]).T.astype(jnp.bfloat16)
+                own = spread(gath[it, 0, 0]).T.astype(jnp.bfloat16)
                 if it == 0:
                     col_x(it, 1).wait_recv()
                     near = rowg[it, 1]
                 else:
                     col_s(it - 1).wait_recv()
                     near = rrecv[it - 1, 0] + rpart[it - 1, 1]
-                lhs[1] = spread(near).T.astype(jnp.bfloat16)
+                near = spread(near).T.astype(jnp.bfloat16)
+                first = jnp.where(col == 0, own, near)
+                second = jnp.where(col == 0, near, own)
+                stack[...] = jnp.concatenate([first, first, second, second], axis=1)
             elif kind == "C":
                 dz, = args
-                zsend[it, dz, 3] = mirror(dz, 3)
+                zsend[it, dz, 3] = mirrored(it, dz, 3)
                 for h in range(2):
                     rs_turn(it, dz, h).start()
             elif kind == "E":
                 dz, d = args
-                zsend[it, dz, d] = mirror(dz, d)
-                if dz == 1:
+                zsend[it, dz, d] = mirrored(it, dz, d)
+                if PAIR and dz == 1:
                     rs_pair(it, d, 0).start()
-                elif dz > 1:
+                elif dz > 0 or not PAIR:
                     rs_plane(it, dz, d, 0).start()
             elif kind == "L":
                 dz, d = args
                 once(rs_turn, "rt", dz, d % 2)
                 zsend[it, dz, d, piece(d)] += zrecv[it, dz, 3, piece(d)]
-                if dz == 1:
+                if PAIR and dz == 1:
                     rs_pair(it, d, 1).start()
                 else:
                     rs_plane(it, dz, d, 1).start()
@@ -401,11 +416,11 @@
                 rs_plane(it, 0, d, q).start()
             elif kind == "M":
                 dz, = args
-                z2send[it, dz] = mirror(dz, 0)
+                z2send[it, dz] = mirrored(it, dz, 0)
             elif kind == "RL":
                 dz, p = args
                 part = piece(p)
-                if dz > 1:
+                if dz > 1 or not PAIR:
                     reduced(dz, 1, p)
                     reduced(dz, 2, 1 - p)
                     z2send[it, dz, part] += zrecv[it, dz, 1, part] + zrecv[it, dz, 2, part]
@@ -424,7 +439,7 @@
                 z2send[it, 0] = pack_tall(unpack_wide(wide, vecs, size))
             elif kind == "AF":
                 dz, d, q = args
-                if dz == 1:
+                if PAIR and dz == 1:
                     gathered(0, d, q)
                     ag_pair_half(it, d, q).start()
                 else:
@@ -450,10 +465,9 @@
                 if place < len(ORDER) - 1:
                     blocked(it, dz, d, it > 0 and task == opening)
         right = spread(gath[it, dz, d]).astype(jnp.bfloat16)
-        mode = access(it, dz, d)
-        rpart[it, 1] = fold_tall(total[1] + term(dz, d, 1, right, mode))
+        rpart[it, 1] = fold_tall(total[1] + terms(dz, d, right, 1)[0])
         col_y(it, 1).start()
-        mine = fold_tall(total[0] + term(dz, d, 0, right, mode)) + z2send[it, 0]
+        mine = fold_tall(total[0] + terms(dz, d, right, 0)[0]) + z2send[it, 0]
         if it < ITERS - 1:
             rpart[it, 0] = mine
             col_s(it).start()
@@ -609,14 +623,14 @@
     count = stiff_tiles.shape[2]
     planes = 4
     lines = rows // planes
-    kept = rows * cols * size * size * 4 <= 16 * 1024 * 1024
+    kept = lines == 4 and cols == 2 and count % CHUNKS == 0 and count <= 64
     block = (size * vecs // LANES, LANES)
     f32 = jnp.float32
     dma = pltpu.SemaphoreType.DMA
     grid = (ITERS, lines, planes)
     return pl.pallas_call(
         functools.partial(kernel, rows, cols, planes, kept),
-        out_shape=jax.ShapeDtypeStruct((vecs, size), f32),
+        out_shape=pltpu.VMEM((vecs, size), f32),
         in_specs=[
             pl.BlockSpec(memory_space=pl.ANY),
             pl.BlockSpec(memory_space=pl.ANY),
@@ -641,8 +655,9 @@
             pltpu.VMEM((ITERS, lines) + block, f32),
             pltpu.VMEM((cols, 2 * vecs, size), jnp.bfloat16),
             pltpu.VMEM((cols, size, 2 * vecs), f32),
-            pltpu.VMEM((rows * cols if kept else 1, 2, size, size), jnp.bfloat16),
-            dma,
+            pltpu.VMEM((count + 1 if kept else 1, 2 * size, size), jnp.bfloat16),
+            pltpu.VMEM((2 * vecs, 4 * size), jnp.bfloat16),
+            dma((CHUNKS,)),
             dma((4,)),
             dma(grid + (2,)), dma(grid + (2,)),
             dma((ITERS, lines, 2)), dma((ITERS, lines, 2)),

time: 42.4 us -> 41.4 us (0.976)
  local copies, waits for them, and re-layouts: 1.47 us -> 0.63 us
    unnamed x1, local copies, waits for them, and re-layouts: 1.47 us -> 0.63 us
where the time goes in v2:
time: 41.4 us; the launch traced here: 41.3 us
  Pallas kernels  40.6 us (98%)
  local copies, waits for them, and re-layouts  0.63 us (2%)
    pallas_call x1, Pallas kernels, local(): pl.pallas_call(functools.partial(kernel, rows, cols, planes, kept), out_s...  40.6 us

profile of v2, /device:TPU:1, one launch (start us, length us, event | category | flops | bytes accessed | tf_op | source)
XLA Modules:
  0.0 41.3 jit_solution(14471469056819812357)
XLA Ops:
  0.0 40.6 %shard_map.46 = f32[64,192]{1,0:T(8,128)S(1)} custom-call(f32[64,192]{1,0:T(8,128)} %bitcast.9, s32[2,32]{1,0:T(2,128)} %bitcast.10, s32[1,32]{1,0:T(1,128)} %bitcast.11, f32[32,192,192]{2,1,0:T(8,128)} %bitcast.8), custom_call_target="tpu_custom_call" | custom-call | tf_op jit(solution)/shard_map/pallas_call | solution.py:631
  40.6 0.6 %copy.6 = f32[192,64]{0,1:T(8,128)} copy(f32[192,64]{0,1:T(8,128)S(1)} %bitcast.7) | data formatting | bytes 98304

commit v3 on v2

--- a/solution.py
+++ b/solution.py
@@ -12,20 +12,22 @@
 LANES = 128
 CHUNKS = 4
 PAIR = True
+RS_DIAG = ()
+AG_DIAG = ()
 ORDER = (
-    ("AP", 2, 0), ("AL", 3, 1), ("AP", 1, 0), ("AP", 1, 1), ("AP", 2, 1), ("AL", 2, 1),
-    ("AL", 1, 1), ("AL", 2, 0), ("LHS",), ("C", 3), ("E", 1, 2), ("C", 2), ("E", 3, 1),
-    ("AL", 1, 0), ("C", 1), ("AL", 3, 0), ("AF", 1, 2, 0), ("AT", 0, 1), ("AF", 1, 1, 0),
-    ("AT", 0, 0), ("E", 3, 2), ("E", 2, 1), ("E", 1, 1), ("D", 0, 1), ("L", 3, 2), ("L", 3, 1),
-    ("AF", 2, 1, 1), ("AF", 1, 1, 1), ("E", 2, 2), ("L", 2, 1), ("L", 2, 2), ("M", 3),
-    ("AF", 2, 1, 0), ("AF", 1, 2, 1), ("AF", 2, 2, 1), ("AF", 2, 2, 0), ("E", 0, 2),
-    ("L", 1, 2), ("AF", 3, 2, 0), ("C", 0), ("L", 1, 1), ("M", 1), ("AF", 3, 1, 0),
-    ("RL", 1, 1), ("AT", 1, 1), ("E", 0, 1), ("AF", 3, 2, 1), ("RL", 3, 0), ("AF", 3, 1, 1),
-    ("S", 2, 0), ("RL", 3, 1), ("M", 2), ("D", 1, 0), ("D", 3, 0), ("RL", 2, 0), ("S", 1, 0),
-    ("RL", 1, 0), ("AT", 1, 0), ("RL", 2, 1), ("AT", 2, 0), ("D", 1, 2), ("AT", 2, 1),
-    ("D", 1, 1), ("AT", 3, 0), ("D", 2, 1), ("AT", 3, 1), ("S", 2, 1), ("S", 1, 1), ("M", 0),
-    ("D", 0, 0), ("D", 3, 2), ("D", 0, 2), ("D", 2, 0), ("D", 2, 2), ("D", 0, 3), ("D", 1, 3),
-    ("D", 3, 1), ("D", 2, 3), ("G",), ("FR",), ("D", 3, 3),
+    ("AP", 2, 0), ("AL", 2, 1), ("AL", 2, 0), ("AL", 1, 0), ("AP", 1, 0), ("AP", 2, 1),
+    ("AP", 1, 1), ("AL", 3, 0), ("LHS",), ("C", 3), ("C", 2), ("AL", 1, 1), ("E", 3, 2),
+    ("AL", 3, 1), ("E", 3, 1), ("C", 0), ("D", 0, 0), ("C", 1), ("E", 1, 1), ("E", 1, 2),
+    ("E", 0, 1), ("L", 3, 1), ("AF", 2, 2, 0), ("AF", 1, 2, 0), ("L", 3, 2), ("AF", 1, 1, 0),
+    ("AF", 1, 1, 1), ("AT", 0, 1), ("AF", 2, 1, 0), ("E", 2, 2), ("E", 2, 1), ("M", 1),
+    ("L", 2, 2), ("M", 2), ("AF", 1, 2, 1), ("AF", 2, 2, 1), ("L", 2, 1), ("L", 1, 1), ("M", 0),
+    ("AF", 3, 1, 1), ("L", 1, 2), ("AF", 3, 2, 0), ("M", 3), ("AF", 3, 1, 0), ("RL", 3, 1),
+    ("RL", 1, 1), ("AT", 2, 1), ("D", 3, 0), ("AF", 3, 2, 1), ("RL", 3, 0), ("AT", 0, 0),
+    ("D", 0, 1), ("AF", 2, 1, 1), ("E", 0, 2), ("AT", 2, 0), ("RL", 2, 0), ("AT", 1, 1),
+    ("S", 1, 0), ("AT", 1, 0), ("S", 2, 0), ("D", 1, 2), ("RL", 1, 0), ("RL", 2, 1),
+    ("D", 2, 2), ("S", 1, 1), ("S", 2, 1), ("AT", 3, 0), ("D", 2, 0), ("AT", 3, 1), ("D", 3, 2),
+    ("D", 0, 2), ("D", 2, 1), ("D", 1, 1), ("D", 0, 3), ("D", 2, 3), ("D", 1, 0), ("D", 3, 1),
+    ("D", 1, 3), ("G",), ("FR",), ("D", 3, 3),
 )
 
 
@@ -157,6 +159,14 @@
         part = piece(d - 1 + q)
         return remote(zsend.at[it, 1, d, part], zrecv.at[it, 1, d, part],
                       r1_send.at[it, 1, d, q], r1_recv.at[it, 1, d, q], line_peer(1))
+
+    def rs_diag(it, dz):
+        return remote(zsend.at[it, dz, 3], zrecv.at[it, dz, 3],
+                      r1_send.at[it, dz, 3, 0], r1_recv.at[it, dz, 3, 0], plane_peer(3))
+
+    def ag_diag(it, dz):
+        return remote(gath.at[it, dz, 0], gath.at[it, dz, 3],
+                      ag_send.at[it, dz, 3, 0], ag_recv.at[it, dz, 3, 0], plane_peer(3))
 
     def rs_line_half(it, dz, p):
         part = piece(p)
@@ -325,23 +335,22 @@
     pl.semaphore_wait(barrier, (lines - 1) + 2 + (cols - 1))
 
     def finish_sends(it):
-        def along(dz, carry):
-            for p in range(2):
-                ag_line_half(it, dz, p).wait_send()
-                rs_line_half(it, dz, p).wait_send()
-            return carry
-
-        def within(dz, carry):
+        for dz in range(lines):
             for h in range(2):
+                if dz > 0:
+                    ag_line_half(it, dz, h).wait_send()
+                    rs_line_half(it, dz, h).wait_send()
                 for d in range(1, 3):
                     ag_plane_half(it, dz, d, h).wait_send()
                     rs_plane(it, dz, d, h).wait_send()
-                ag_turn(it, dz, h).wait_send()
-                rs_turn(it, dz, h).wait_send()
-            return carry
-
-        lax.fori_loop(1, lines, along, 0)
-        lax.fori_loop(0, lines, within, 0)
+                if dz not in AG_DIAG:
+                    ag_turn(it, dz, h).wait_send()
+                if dz not in RS_DIAG:
+                    rs_turn(it, dz, h).wait_send()
+            if dz in AG_DIAG:
+                ag_diag(it, dz).wait_send()
+            if dz in RS_DIAG:
+                rs_diag(it, dz).wait_send()
 
     def ordered(it):
         arrived = set()
@@ -387,15 +396,19 @@
             elif kind == "C":
                 dz, = args
                 zsend[it, dz, 3] = mirrored(it, dz, 3)
-                for h in range(2):
-                    rs_turn(it, dz, h).start()
+                if dz in RS_DIAG:
+                    rs_diag(it, dz).start()
+                else:
+                    for h in range(2):
+                        rs_turn(it, dz, h).start()
             elif kind == "E":
                 dz, d = args
                 zsend[it, dz, d] = mirrored(it, dz, d)
-                if PAIR and dz == 1:
-                    rs_pair(it, d, 0).start()
-                elif dz > 0 or not PAIR:
-                    rs_plane(it, dz, d, 0).start()
+                for q in range(2 if dz in RS_DIAG else 1):
+                    if PAIR and dz == 1:
+                        rs_pair(it, d, q).start()
+                    elif dz > 0 or not PAIR:
+                        rs_plane(it, dz, d, q).start()
             elif kind == "L":
                 dz, d = args
                 once(rs_turn, "rt", dz, d % 2)
@@ -409,7 +422,7 @@
                 part = piece(d - 1 + q)
                 once(lambda it, dz, d, q: rs_pair(it, d, q), "rp", 1, d, q)
                 more = zrecv[it, 1, d, part]
-                if q == 1:
+                if q == 1 and 0 not in RS_DIAG:
                     once(rs_turn, "rt", 0, d % 2)
                     more = more + zrecv[it, 0, 3, part]
                 zsend[it, 0, d, part] += more
@@ -424,12 +437,18 @@
                     reduced(dz, 1, p)
                     reduced(dz, 2, 1 - p)
                     z2send[it, dz, part] += zrecv[it, dz, 1, part] + zrecv[it, dz, 2, part]
+                if dz in RS_DIAG:
+                    once(rs_diag, "rd", dz)
+                    z2send[it, dz, part] += zrecv[it, dz, 3, part]
                 rs_line_half(it, dz, p).start()
             elif kind == "G":
                 for d in range(1, 3):
                     for q in range(2):
                         reduced(0, d, q)
                 z2send[it, 0] += zrecv[it, 0, 1] + zrecv[it, 0, 2]
+                if 0 in RS_DIAG:
+                    once(rs_diag, "rd", 0)
+                    z2send[it, 0] += zrecv[it, 0, 3]
             elif kind == "FR":
                 wide = z2send[it, 0]
                 for dz in range(1, lines):
@@ -449,6 +468,12 @@
                 dz, h = args
                 gathered(dz, 1 + h, 0)
                 ag_turn(it, dz, h).start()
+            elif kind == "AD":
+                dz, = args
+                if dz > 0:
+                    for p in range(2):
+                        once(ag_line_half, "al", dz, p)
+                ag_diag(it, dz).start()
             elif it > 0 or args != (0, 0):
                 dz, d = args
                 if place == len(ORDER) - 1 and it == ITERS - 1:
@@ -459,6 +484,8 @@
                 elif d in (1, 2):
                     for q in range(2):
                         gathered(dz, d, q)
+                elif d == 3 and dz in AG_DIAG:
+                    once(ag_diag, "ad", dz)
                 elif d == 3:
                     for h in range(2):
                         once(ag_turn, "at", dz, h)

time: 41.4 us -> 40.7 us (0.983)
  Pallas kernels: 40.6 us -> 40 us
    pallas_call x1, Pallas kernels: 40.6 us -> 40 us  [local(): pl.pallas_call(functools.partial(kernel, rows, cols, planes, kept), out_s...]
where the time goes in v3:
time: 40.7 us; the launch traced here: 40.6 us
  Pallas kernels  40 us (98%)
  local copies, waits for them, and re-layouts  0.63 us (2%)
    pallas_call x1, Pallas kernels, local(): pl.pallas_call(functools.partial(kernel, rows, cols, planes, kept), out_s...  40 us

profile of v3, /device:TPU:1, one launch (start us, length us, event | category | flops | bytes accessed | tf_op | source)
XLA Modules:
  0.0 40.6 jit_solution(5587884169942876595)
XLA Ops:
  0.0 40.0 %shard_map.46 = f32[64,192]{1,0:T(8,128)S(1)} custom-call(f32[64,192]{1,0:T(8,128)} %bitcast.9, s32[2,32]{1,0:T(2,128)} %bitcast.10, s32[1,32]{1,0:T(1,128)} %bitcast.11, f32[32,192,192]{2,1,0:T(8,128)} %bitcast.8), custom_call_target="tpu_custom_call" | custom-call | tf_op jit(solution)/shard_map/pallas_call | solution.py:658
  40.0 0.6 %copy.6 = f32[192,64]{0,1:T(8,128)} copy(f32[192,64]{0,1:T(8,128)S(1)} %bitcast.7) | data formatting | bytes 98304

commit v4 on v3

--- a/solution.py
+++ b/solution.py
@@ -476,8 +476,6 @@
                 ag_diag(it, dz).start()
             elif it > 0 or args != (0, 0):
                 dz, d = args
-                if place == len(ORDER) - 1 and it == ITERS - 1:
-                    finish_sends(it)
                 if d == 0 and dz > 0:
                     for p in range(2):
                         once(ag_line_half, "al", dz, p)
@@ -498,6 +496,8 @@
         if it < ITERS - 1:
             rpart[it, 0] = mine
             col_s(it).start()
+        if it == ITERS - 1:
+            finish_sends(it)
         col_y(it, 1).wait_recv()
         return mine + rrecv[it, 1]
 

time: 40.7 us -> 40.7 us (level)
  no operation moved by 1% of the time
where the time goes in v4:
time: 40.7 us; the launch traced here: 40.6 us
  Pallas kernels  39.9 us (98%)
  local copies, waits for them, and re-layouts  0.63 us (2%)
    pallas_call x1, Pallas kernels, local(): pl.pallas_call(functools.partial(kernel, rows, cols, planes, kept), out_s...  39.9 us

profile of v4, /device:TPU:1, one launch (start us, length us, event | category | flops | bytes accessed | tf_op | source)
XLA Modules:
  0.0 40.6 jit_solution(3094888432439014174)
XLA Ops:
  0.0 39.9 %shard_map.46 = f32[64,192]{1,0:T(8,128)S(1)} custom-call(f32[64,192]{1,0:T(8,128)} %bitcast.9, s32[2,32]{1,0:T(2,128)} %bitcast.10, s32[1,32]{1,0:T(1,128)} %bitcast.11, f32[32,192,192]{2,1,0:T(8,128)} %bitcast.8), custom_call_target="tpu_custom_call" | custom-call | tf_op jit(solution)/shard_map/pallas_call | solution.py:658
  39.9 0.6 %copy.6 = f32[192,64]{0,1:T(8,128)} copy(f32[192,64]{0,1:T(8,128)S(1)} %bitcast.7) | data formatting | bytes 98304
